TPU v7x, 128 devices: a whole 4x4x4 slice. The times are simulated.
128 devices in a mesh: scene: 8 (over y, core), frame: 16 (over z, x).
Axes of the slice: x: 4, y: 4, z: 4, core: 2. Of those that a mesh axis runs over, the one named last changes fastest.
Arguments:
- occupancy: bfloat16 [8, 64, 64, 2048], P('scene', 'frame'), may hold values from -6 to 6
- scene_lengths: int32 [8], P('scene'), may hold values from 8 to 64, as said below
- conv1_weight: bfloat16 [128, 1728], replicated, may hold values from -0.15625 to 0.15625
- conv2_weight: bfloat16 [256, 3456], replicated, may hold values from -0.109375 to 0.109375
- temporal_weight: bfloat16 [3, 256, 256], replicated, may hold values from -0.21875 to 0.21875
- query_weight: bfloat16 [256, 256], replicated
- key_weight: bfloat16 [256, 256], replicated
- value_weight: bfloat16 [256, 256], replicated, may hold values from -0.375 to 0.375
- out_weight: bfloat16 [256, 256], replicated, may hold values from -0.375 to 0.375
Outputs:
- encoded: bfloat16 [8, 64, 256, 512], P('scene', 'frame')
- kl_loss: float32 [], replicated
Inputs may be any that keep to these rules, and one draw needn't show every extreme that they name: `scene_lengths`: non-decreasing along the scenes; the first scene has exactly 8 frames with data and the last exactly 64.
All inputs are finite; a program needn't handle non-finite values.
Results may differ from a plain program's by a relative error of at most 0.011.
Values may be sent and summed in bfloat16 or wider, within the bound.
A program may use at most 192 MiB of HBM per device.

v0:
```python
import jax
import jax.numpy as jnp
from jax import lax
from jax.sharding import PartitionSpec as P

CIN = 64
C1 = 128
C2 = 256
HEADS = 4
HD = 64
HI = 16
ZD = 8
CELLS = 512
NORM_EPS = 1e-06


def extended(cells, sides, width):
    for axis, dim in sides:
        count = lax.axis_size(axis)
        ends = count - 1
        head = lax.slice_in_dim(cells, 0, width, axis=dim)
        tail = lax.slice_in_dim(cells, cells.shape[dim] - width, cells.shape[dim], axis=dim)
        cells = jnp.concatenate(
            [
                lax.ppermute(tail, axis, [(i, (i + 1) % count) for i in range(ends)]),
                cells,
                lax.ppermute(head, axis, [((i + 1) % count, i) for i in range(ends)]),
            ],
            axis=dim,
        )
    return cells


def spatial_conv(voxels, weight, channels_in, stride):
    channels_out = weight.shape[0]
    kernel = weight.reshape(channels_out, channels_in, 3, 3, 3)
    return lax.conv_general_dilated(
        voxels,
        kernel,
        (stride, stride, 1),
        ((1, 1), (1, 1), (1, 1)),
        dimension_numbers=("NCDHW", "OIDHW", "NCDHW"),
        preferred_element_type=jnp.float32,
    )


def mix_channels(weight, maps):
    return jnp.einsum("oc,fcn->fon", weight, maps, preferred_element_type=jnp.float32)


def temporal_block(padded, second_maps, temporal_weight):
    count_frames = second_maps.shape[0]
    temporal_sum = mix_channels(temporal_weight[0], padded[0:count_frames])
    for tap in range(1, 3):
        temporal_sum = temporal_sum + mix_channels(
            temporal_weight[tap], padded[tap : tap + count_frames]
        )
    residual_maps = (second_maps.astype(jnp.float32) + jax.nn.silu(temporal_sum)).astype(
        jnp.bfloat16
    )
    return residual_maps.astype(jnp.float32)


def project_rows(residual_f, query_weight, key_weight, value_weight):
    count_frames = residual_f.shape[0]
    count_cells = residual_f.shape[2]
    normed = (
        residual_f * lax.rsqrt(jnp.mean(residual_f * residual_f, axis=1, keepdims=True) + NORM_EPS)
    ).astype(jnp.bfloat16)
    queries = (
        mix_channels(query_weight, normed)
        .astype(jnp.bfloat16)
        .reshape(count_frames, HEADS, HD, count_cells)
    )
    key_rows = (
        mix_channels(key_weight, normed)
        .astype(jnp.bfloat16)
        .reshape(count_frames, HEADS, HD, count_cells)
    )
    value_rows = (
        mix_channels(value_weight, normed)
        .astype(jnp.bfloat16)
        .reshape(count_frames, HEADS, HD, count_cells)
    )
    return (queries, key_rows, value_rows)


def finish_rows(residual_f, attended, out_weight, valid_rows):
    count_frames = residual_f.shape[0]
    count_cells = residual_f.shape[2]
    out_full = residual_f + mix_channels(
        out_weight, attended.reshape(count_frames, C2, count_cells)
    )
    return (out_full * valid_rows[:, None, None]).astype(jnp.bfloat16)


def shards(
    occupancy,
    scene_lengths,
    conv1_weight,
    conv2_weight,
    temporal_weight,
    query_weight,
    key_weight,
    value_weight,
    out_weight,
):
    f_dev = occupancy.shape[1]
    length = scene_lengths[0]
    first_frame = lax.axis_index("frame") * f_dev
    frame_ids = first_frame + jnp.arange(f_dev, dtype=jnp.int32)
    valid_rows = (frame_ids < length).astype(jnp.float32)
    voxels = occupancy[0].reshape(f_dev, CIN, HI, HI, ZD)
    first_maps = jax.nn.silu(spatial_conv(voxels, conv1_weight, CIN, 2)).astype(jnp.bfloat16)
    second_full = jax.nn.silu(spatial_conv(first_maps, conv2_weight, C1, 1))
    second_maps = (second_full.reshape(f_dev, C2, CELLS) * valid_rows[:, None, None]).astype(
        jnp.bfloat16
    )
    padded = extended(second_maps, (("frame", 0),), 1)
    residual_f = temporal_block(padded, second_maps, temporal_weight)
    queries, key_rows, value_rows = project_rows(residual_f, query_weight, key_weight, value_weight)
    running_max = jnp.full((f_dev, HEADS, CELLS), -1e30, jnp.float32)
    panel_keys = lax.all_gather(key_rows, "frame", axis=0, tiled=True)
    panel_values = lax.all_gather(value_rows, "frame", axis=0, tiled=True)
    count_keys = panel_keys.shape[0]
    scores = jnp.einsum(
        "qhdc,khdc->qkhc", queries, panel_keys, preferred_element_type=jnp.float32
    ) * HD ** (-0.5)
    key_mask = (jnp.arange(count_keys) < length)[None, :, None, None]
    scores = jnp.where(key_mask, scores, -1e30)
    new_max = jnp.maximum(running_max, jnp.max(scores, axis=1))
    raw_weights = jnp.where(key_mask, jnp.exp(scores - new_max[:, None]), 0.0)
    new_sum = jnp.sum(raw_weights, axis=1)
    addition = jnp.einsum(
        "qkhc,khdc->qhdc",
        raw_weights.astype(jnp.bfloat16),
        panel_values,
        preferred_element_type=jnp.float32,
    )
    attended = (addition / new_sum[:, :, None, :]).astype(jnp.bfloat16)
    encoded = finish_rows(residual_f, attended, out_weight, valid_rows)
    squares = jnp.sum(jnp.square(encoded.astype(jnp.float32)))
    grand_total = lax.psum(squares, ("scene", "frame"))
    slot_count = float(lax.axis_size("scene") * lax.axis_size("frame") * f_dev * CELLS * C2)
    kl_loss = 0.5 * grand_total / slot_count
    return (encoded[None], kl_loss)


def solution(mesh):
    placed = (P("scene", "frame", None, None), P("scene"), P(), P(), P(), P(), P(), P(), P())
    return jax.shard_map(
        shards,
        mesh=mesh,
        in_specs=placed,
        out_specs=(P("scene", "frame", None, None), P()),
        check_vma=False,
    )
```

profile of v0, /device:TPU:1, one launch (start us, length us, event | category | flops | bytes accessed | tf_op | source)
XLA Modules:
  0.0 420.5 jit_solution(17460069256639030074)
XLA Ops:
  7.2 0.0 copy-start
  7.2 0.0 all-gather.5.cloned.1.call-start
  7.9 2.6 copy.62
  10.5 0.0 copy-start.3
  10.6 2.9 reshape.49
  13.4 0.0 copy-done.3
  13.4 1.1 copy.59
  14.5 1.5 reshape.48
  16.0 0.0 copy-start.1
  16.0 5.0 %fusion.28 = bf16[4,128,8,8,8]{1,0,4,3,2:T(4,128)(2,1)S(1)} fusion(bf16[4,64,16,16,8]{1,4,3,2,0:T(8,128)(2,1)S(1)} %bitcast.90, bf16[128,64,3,3,3]{0,4,3,2,1:T(4,128)(2,1)S(1)} %reshape.48), kind=kOutput, calls=%fused_computation.44 | convolution fusion | flops 764018688 | bytes 2015232 | tf_op jit(solution)/shard_map/conv_general_dilated | solution.py:37
  21.0 0.0 copy-done.1
  21.0 7.9 %multiply_convert_fusion = (bf16[4,256,8,8,8]{1,0,4,3,2:T(4,128)(2,1)S(1)}, f32[4,256,8,8,8]{1,0,4,3,2:T(4,128)}) fusion(f32[4]{0:T(128)S(1)} %compare_convert_fusion, bf16[4,128,8,8,8]{1,0,4,3,2:T(4,128)(2,1)S(1)} %fusion.28, bf16[256,128,3,3,3]{0,4,3,2,1:T(4,128)(2,1)S(1)} %copy-done.1), kind=kOutput, calls=%fused_computation.24 | convolution fusion | flops 2794455040 | bytes 5439504 | tf_op jit(solution)/shard_map/conv_general_dilated | solution.py:37
  28.9 1.9 copy.64
  30.8 0.0 copy-start.4
  30.8 0.3 multiply_convert_fusion.1
  31.2 4.0 collective-permute-start
  35.1 1.5 collective-permute-start.1
  36.6 0.0 copy-done.4
  36.6 0.5 fusion.26
  37.1 3.0 collective-permute-done
  40.1 0.4 fusion.24
  40.5 0.0 copy-start.5
  40.5 3.4 collective-permute-done.1
  43.9 1.1 fusion.2
  44.9 0.0 copy-start.6
  45.0 0.0 copy-done.5
  45.0 1.4 convolution_convert_fusion.1
  46.4 0.0 all-gather.5.cloned.1.call-update
  46.4 0.0 all-gather.3.cloned.1.call-start
  46.5 0.0 copy-done.6
  46.5 1.4 convolution_convert_fusion.2
  47.9 0.0 all-gather.3.cloned.1.call-update
  48.0 0.5 convolution_convert_fusion
  48.4 2.5 copy.67
  50.9 112.4 %all-gather.5.cloned.1.call-done = bf16[64,4,64,512]{3,2,1,0:T(8,128)(2,1)} async-done(((bf16[4,4,64,512]{3,2,1,0:T(8,128)(2,1)}), bf16[64,4,64,512]{3,2,1,0:T(8,128)(2,1)}) %all-gather.5.cloned.1.call-update) | async-done | bytes 16777232 | tf_op jit(solution)/shard_map/all_gather | solution.py:123
  163.3 46.8 %copy.66 = bf16[64,4,64,512]{2,0,3,1:T(8,128)(2,1)} copy(bf16[64,4,64,512]{3,2,1,0:T(8,128)(2,1)} %all-gather.5.cloned.1.call-done) | data formatting | bytes 33554432 | tf_op jit(solution)/shard_map/all_gather | solution.py:123
  210.1 24.4 %bitcast_reduce_fusion = (f32[4,4,512]{0,2,1:T(8,128)}, f32[4,512,64,4]{2,3,1,0:T(4,128)}) fusion(pred[64]{0:T(512)(128)(4,1)S(1)} %iota_compare_fusion, bf16[64,4,64,512]{2,0,3,1:T(8,128)(2,1)} %copy.66, bf16[4,4,64,512]{2,0,3,1:T(4,128)(2,1)S(1)} %copy-done.2), kind=kOutput, calls=%fused_computation.1 | convolution fusion | flops 68673536 | bytes 19955776 | tf_op jit(solution)/shard_map/qhdc,khdc->qkhc/dot_general | solution.py:126
  234.5 1.4 broadcast_maximum_fusion
  235.9 30.0 %fusion.20 = f32[4,4,512]{0,2,1:T(8,128)S(1)} fusion(f32[4,4,512]{0,2,1:T(8,128)S(1)} %broadcast_maximum_fusion, f32[4,512,64,4]{2,3,1,0:T(4,128)} %get-tuple-element.9, pred[64]{0:T(512)(128)(4,1)S(1)} %iota_compare_fusion), kind=kLoop, calls=%fused_computation.34 | loop fusion | flops 2613248 | bytes 2162752 | tf_op jit(solution)/shard_map/reduce_sum | solution.py:133
  265.9 0.3 copy.70
  266.2 10.9 %all-gather.3.cloned.1.call-done = bf16[64,4,64,512]{3,2,1,0:T(8,128)(2,1)} async-done(((bf16[4,4,64,512]{3,2,1,0:T(8,128)(2,1)}), bf16[64,4,64,512]{3,2,1,0:T(8,128)(2,1)}) %all-gather.3.cloned.1.call-update) | async-done | bytes 16777232 | tf_op jit(solution)/shard_map/all_gather | solution.py:124
  277.1 46.6 %copy.68 = bf16[64,4,64,512]{2,0,3,1:T(8,128)(2,1)} copy(bf16[64,4,64,512]{3,2,1,0:T(8,128)(2,1)} %all-gather.3.cloned.1.call-done) | data formatting | bytes 33554432 | tf_op jit(solution)/shard_map/all_gather | solution.py:124
  323.7 17.5 %fusion.11 = f32[4,512,64,4]{2,3,1,0:T(4,128)} fusion(bf16[64,4,64,512]{2,0,3,1:T(8,128)(2,1)} %copy.68, f32[4,512,64,4]{2,3,1,0:T(4,128)} %get-tuple-element.9, f32[4,4,512]{0,2,1:T(8,128)S(1)} %broadcast_maximum_fusion, pred[64]{0:T(512)(128)(4,1)S(1)} %iota_compare_fusion), kind=kOutput, calls=%fused_computation.22 | convolution fusion | flops 69730304 | bytes 21004352 | tf_op jit(solution)/shard_map/qkhc,khdc->qhdc/dot_general | solution.py:134
  341.2 3.5 copy.69
  344.7 0.3 fusion.6
  345.0 0.0 copy-done
  345.0 2.3 multiply_reduce_fusion
  347.3 64.6 %psum.7 = f32[]{:T(128)} all-reduce(f32[]{:T(128)} %get-tuple-element.10), channel_id=1, replica_groups=mesh['scene'=8,'frame'=16] {'scene','frame'}, use_global_device_ids=true, to_apply=%region_4.5 | all-reduce | flops 1 | bytes 8 | tf_op jit(solution)/shard_map/psum | solution.py:143
  (8 shorter events, 0.1 us)
Async XLA Ops:
  7.2 337.9 %copy-start = (bf16[256,256]{1,0:T(8,128)(2,1)S(1)}, bf16[256,256]{1,0:T(8,128)(2,1)}, u32[]{:S(2)}) copy-start(bf16[256,256]{1,0:T(8,128)(2,1)} %param.17) | copy-start | bytes 393220
  7.2 156.1 %all-gather.5.cloned.1.call-start = ((), (), s32[]{:S(2)}) async-start(), calls=%async_computation.1 | async-start | bytes 17825792 | tf_op jit(solution)/shard_map/all_gather | solution.py:123
  10.5 2.9 copy-start.3
  16.0 5.0 %copy-start.1 = (bf16[256,128,3,3,3]{0,4,3,2,1:T(4,128)(2,1)S(1)}, bf16[256,128,3,3,3]{0,4,3,2,1:T(4,128)(2,1)}, u32[]{:S(2)}) copy-start(bf16[256,128,3,3,3]{0,4,3,2,1:T(4,128)(2,1)} %reshape.49) | copy-start | bytes 5308420
  30.8 5.8 %copy-start.4 = (bf16[3,256,256]{2,1,0:T(8,128)(2,1)S(1)}, bf16[3,256,256]{2,1,0:T(8,128)(2,1)}, u32[]{:S(2)}) copy-start(bf16[3,256,256]{2,1,0:T(8,128)(2,1)} %param.13) | copy-start | bytes 1179652
  31.2 8.9 %collective-permute-start = (bf16[1,256,512]{2,1,0:T(8,128)(2,1)S(1)}, bf16[1,256,512]{2,1,0:T(8,128)(2,1)S(1)}, u32[]{:S(2)}, u32[]{:S(2)}) collective-permute-start(bf16[1,256,512]{2,1,0:T(8,128)(2,1)S(1)} %get-tuple-element.3), channel_id=1, source_target_pairs={{0,1},{1,2},{2,3},{3,4},{4,5},{5,6},{6,7},{7,8},{8,9},{9,10},{10,1... | collective-permute-start | bytes 786440 | tf_op jit(solution)/shard_map/ppermute | solution.py:25
  35.1 8.7 %collective-permute-start.1 = (bf16[1,256,512]{2,1,0:T(8,128)(2,1)S(1)}, bf16[1,256,512]{2,1,0:T(8,128)(2,1)S(1)}, u32[]{:S(2)}, u32[]{:S(2)}) collective-permute-start(bf16[1,256,512]{2,1,0:T(8,128)(2,1)S(1)} %get-tuple-element.2), channel_id=1, source_target_pairs={{1,0},{2,1},{3,2},{4,3},{5,4},{6,5},{7,6},{8,7},{9,8},{10,9},{11,1... | collective-permute-start | bytes 786440 | tf_op jit(solution)/shard_map/ppermute | solution.py:27
  40.5 4.5 %copy-start.5 = (bf16[256,256]{1,0:T(8,128)(2,1)S(1)}, bf16[256,256]{1,0:T(8,128)(2,1)}, u32[]{:S(2)}) copy-start(bf16[256,256]{1,0:T(8,128)(2,1)} %param.15) | copy-start | bytes 393220
  44.9 1.5 copy-start.6
  46.4 1.6 copy-start.7
  46.4 230.7 %all-gather.3.cloned.1.call-start = ((), (), s32[]{:S(2)}) async-start(), calls=%async_computation | async-start | bytes 17825792 | tf_op jit(solution)/shard_map/all_gather | solution.py:124
  50.9 159.2 %copy-start.2 = (bf16[4,4,64,512]{2,0,3,1:T(4,128)(2,1)S(1)}, bf16[4,4,64,512]{2,0,3,1:T(4,128)(2,1)}, u32[]{:S(2)}) copy-start(bf16[4,4,64,512]{2,0,3,1:T(4,128)(2,1)} %copy.67) | copy-start | bytes 3145732
Sparse Core Ops, SparseCore 0:
  46.6 116.7 all-gather.4
  166.0 111.0 all-gather.2
where the time goes:
time: 423 us; the launch traced here: 421 us
  waiting for transfers between devices  130 us (31%)
  local copies, waits for them, and re-layouts  110 us (26%)
  blocking collectives  64.6 us (15%)
  matrix products  62.2 us (15%)
  other arithmetic  32 us (8%)
  between operations  16.7 us (4%)
  starting transfers between devices  5.51 us (1%)
    all_gather x1, waiting for transfers between devices, shards(): panel_keys = lax.all_gather(key_rows, 'frame', axis=0, tiled=True)  112 us
    psum x1, blocking collectives, shards(): grand_total = lax.psum(squares, ('scene', 'frame'))  64.6 us
    all_gather x1, local copies, waits for them, and re-layouts, shards(): panel_keys = lax.all_gather(key_rows, 'frame', axis=0, tiled=True)  46.8 us
    all_gather x1, local copies, waits for them, and re-layouts, shards(): panel_values = lax.all_gather(value_rows, 'frame', axis=0, tiled=True)  46.6 us
    reduce_sum x1, other arithmetic, shards(): new_sum = jnp.sum(raw_weights, axis=1)  30 us
    dot_general x1, matrix products, shards(): jnp.einsum('qhdc,khdc->qkhc', queries, panel_keys, preferred_element_type...  24.4 us
    dot_general x1, matrix products, shards(): jnp.einsum('qkhc,khdc->qhdc', raw_weights.astype(jnp.bfloat16), panel_val...  17.5 us
    conv_general_dilated x2, matrix products, spatial_conv(): lax.conv_general_dilated(voxels, kernel, (stride, stride, 1), ((1, 1), (1...  12.8 us
  transfers between devices with their start and end apart: 4, of which 4 were waited for; matrix products, arithmetic and copies ran while one was open for 26% of the time, Pallas kernels for 0%

commit v1 on v0

--- a/solution.py
+++ b/solution.py
@@ -120,7 +120,10 @@
     residual_f = temporal_block(padded, second_maps, temporal_weight)
     queries, key_rows, value_rows = project_rows(residual_f, query_weight, key_weight, value_weight)
     running_max = jnp.full((f_dev, HEADS, CELLS), -1e30, jnp.float32)
-    panel_keys = lax.all_gather(key_rows, "frame", axis=0, tiled=True)
+    size = lax.axis_size("frame")
+    blocks = jnp.stack([key_rows for _ in range(size)])
+    blocks = lax.all_to_all(blocks, "frame", split_axis=0, concat_axis=0)
+    panel_keys = jnp.concatenate(blocks, axis=0)
     panel_values = lax.all_gather(value_rows, "frame", axis=0, tiled=True)
     count_keys = panel_keys.shape[0]
     scores = jnp.einsum(

time: 423 us -> 628 us (1.48)
  waiting for transfers between devices: 130 us -> 313 us
  local copies, waits for them, and re-layouts: 110 us -> 121 us
  starting transfers between devices: 5.51 us -> 15 us
    all_to_all x0 -> x1, waiting for transfers between devices: none -> 307 us  [shards(): blocks = lax.all_to_all(blocks, 'frame', split_axis=0, concat_axis=0)]
    all_gather x1 -> x0, waiting for transfers between devices: 112 us -> none  [shards(): panel_keys = lax.all_gather(key_rows, 'frame', axis=0, tiled=True)]
    all_to_all x0 -> x1, local copies, waits for them, and re-layouts: none -> 52 us  [shards(): blocks = lax.all_to_all(blocks, 'frame', split_axis=0, concat_axis=0)]
    all_gather x1 -> x0, local copies, waits for them, and re-layouts: 46.8 us -> none  [shards(): panel_keys = lax.all_gather(key_rows, 'frame', axis=0, tiled=True)]
    all_gather x1, waiting for transfers between devices: 10.9 us -> 0.01 us  [shards(): panel_values = lax.all_gather(value_rows, 'frame', axis=0, tiled=True)]
    all_to_all x0 -> x1, starting transfers between devices: none -> 9.49 us  [shards(): blocks = lax.all_to_all(blocks, 'frame', split_axis=0, concat_axis=0)]
  transfers between devices with their start and end apart: 4 -> 4, of which waited for: 4 -> 3; matrix products, arithmetic and copies ran while one was open for 26% -> 19% of each run, Pallas kernels for 0% -> 0%
where the time goes in v1:
time: 628 us; the launch traced here: 625 us
  waiting for transfers between devices  313 us (50%)
  local copies, waits for them, and re-layouts  121 us (19%)
  blocking collectives  66.6 us (11%)
  matrix products  61.2 us (10%)
  other arithmetic  32 us (5%)
  between operations  16.7 us (3%)
  starting transfers between devices  15 us (2%)
    all_to_all x1, waiting for transfers between devices, shards(): blocks = lax.all_to_all(blocks, 'frame', split_axis=0, concat_axis=0)  307 us
    psum x1, blocking collectives, shards(): grand_total = lax.psum(squares, ('scene', 'frame'))  66.6 us
    all_to_all x1, local copies, waits for them, and re-layouts, shards(): blocks = lax.all_to_all(blocks, 'frame', split_axis=0, concat_axis=0)  52 us
    all_gather x1, local copies, waits for them, and re-layouts, shards(): panel_values = lax.all_gather(value_rows, 'frame', axis=0, tiled=True)  46.7 us
    reduce_sum x1, other arithmetic, shards(): new_sum = jnp.sum(raw_weights, axis=1)  30 us
    dot_general x1, matrix products, shards(): jnp.einsum('qhdc,khdc->qkhc', queries, panel_keys, preferred_element_type...  24.3 us
    dot_general x1, matrix products, shards(): jnp.einsum('qkhc,khdc->qhdc', raw_weights.astype(jnp.bfloat16), panel_val...  17.5 us
    conv_general_dilated x2, matrix products, spatial_conv(): lax.conv_general_dilated(voxels, kernel, (stride, stride, 1), ((1, 1), (1...  12.8 us
  transfers between devices with their start and end apart: 4, of which 3 were waited for; matrix products, arithmetic and copies ran while one was open for 19% of the time, Pallas kernels for 0%

profile of v1, /device:TPU:1, one launch (start us, length us, event | category | flops | bytes accessed | tf_op | source)
XLA Modules:
  0.0 625.3 jit_solution(18419421912157549353)
XLA Ops:
  7.2 0.0 copy-start
  7.2 0.0 all-gather.2.cloned.1.call-start
  7.9 2.6 copy.62
  10.5 0.0 copy-start.3
  10.6 2.9 reshape.51
  13.4 0.0 copy-done.3
  13.4 1.1 copy.59
  14.5 1.5 reshape.50
  16.0 0.0 copy-start.1
  16.0 5.0 fusion.28
  21.0 0.0 copy-done.1
  21.0 7.8 %multiply_convert_fusion = (bf16[4,256,8,8,8]{1,0,4,3,2:T(4,128)(2,1)S(1)}, f32[4,256,8,8,8]{1,0,4,3,2:T(4,128)}) fusion(f32[4]{0:T(128)S(1)} %compare_convert_fusion, bf16[4,128,8,8,8]{1,0,4,3,2:T(4,128)(2,1)S(1)} %fusion.28, bf16[256,128,3,3,3]{0,4,3,2,1:T(4,128)(2,1)S(1)} %copy-done.1), kind=kOutput, calls=%fused_computation.24 | convolution fusion | flops 2794455040 | bytes 5439504 | tf_op jit(solution)/shard_map/conv_general_dilated | solution.py:37
  28.8 1.9 copy.64
  30.8 0.0 copy-start.4
  30.8 0.3 multiply_convert_fusion.1
  31.2 4.0 collective-permute-start
  35.1 1.5 collective-permute-start.1
  36.6 0.0 copy-done.4
  36.6 0.5 fusion.26
  37.1 3.0 collective-permute-done
  40.1 0.4 fusion.24
  40.5 0.0 copy-start.5
  40.5 3.4 collective-permute-done.1
  43.9 1.1 fusion.2
  44.9 0.0 copy-start.6
  45.0 0.0 copy-done.5
  45.0 1.4 convolution_convert_fusion.2
  46.4 0.0 all-gather.2.cloned.1.call-update
  46.4 0.0 copy-done.6
  46.4 0.5 convolution_convert_fusion.1
  46.9 5.9 stack.3
  52.8 9.5 %all-to-all-start = ((bf16[16,4,4,64,512]{4,3,2,1,0:T(8,128)(2,1)}), bf16[16,4,4,64,512]{4,3,2,1,0:T(8,128)(2,1)}, u32[]{:S(2)}, u32[]{:S(2)}) async-start(bf16[16,4,4,64,512]{4,3,2,1,0:T(8,128)(2,1)} %stack.3), calls=%async_computation | async-start | bytes 33554432 | tf_op jit(solution)/shard_map/all_to_all | solution.py:125
  62.4 0.5 convolution_convert_fusion
  62.8 2.5 copy.67
  65.3 306.6 %all-to-all-done = bf16[16,4,4,64,512]{4,3,2,1,0:T(8,128)(2,1)} async-done(((bf16[16,4,4,64,512]{4,3,2,1,0:T(8,128)(2,1)}), bf16[16,4,4,64,512]{4,3,2,1,0:T(8,128)(2,1)}, u32[]{:S(2)}, u32[]{:S(2)}) %all-to-all-start) | async-done | bytes 16777248 | tf_op jit(solution)/shard_map/all_to_all | solution.py:125
  371.9 52.0 %copy.66 = bf16[16,4,4,64,512]{3,1,0,4,2:T(4,128)(2,1)} copy(bf16[16,4,4,64,512]{4,3,2,1,0:T(8,128)(2,1)} %all-to-all-done) | data formatting | bytes 33554432 | tf_op jit(solution)/shard_map/all_to_all | solution.py:125
  423.9 0.0 copy-done.2
  423.9 24.3 %bitcast_reduce_fusion = (f32[4,4,512]{0,2,1:T(8,128)}, f32[4,512,64,4]{2,3,1,0:T(4,128)}) fusion(pred[64]{0:T(512)(128)(4,1)S(1)} %iota_compare_fusion, bf16[64,4,64,512]{2,0,3,1:T(8,128)(2,1)} %bitcast.88, bf16[4,4,64,512]{2,0,3,1:T(4,128)(2,1)S(1)} %copy-done.2), kind=kOutput, calls=%fused_computation.1 | convolution fusion | flops 68673536 | bytes 19955776 | tf_op jit(solution)/shard_map/qhdc,khdc->qkhc/dot_general | solution.py:129
  448.2 1.3 broadcast_maximum_fusion
  449.5 30.0 %fusion.20 = f32[4,4,512]{0,2,1:T(8,128)S(1)} fusion(f32[4,4,512]{0,2,1:T(8,128)S(1)} %broadcast_maximum_fusion, f32[4,512,64,4]{2,3,1,0:T(4,128)} %get-tuple-element.9, pred[64]{0:T(512)(128)(4,1)S(1)} %iota_compare_fusion), kind=kLoop, calls=%fused_computation.34 | loop fusion | flops 2613248 | bytes 2162752 | tf_op jit(solution)/shard_map/reduce_sum | solution.py:136
  479.6 0.3 copy.70
  479.9 46.7 %copy.68 = bf16[64,4,64,512]{2,0,3,1:T(8,128)(2,1)} copy(bf16[64,4,64,512]{3,2,1,0:T(8,128)(2,1)} %all-gather.2.cloned.1.call-done) | data formatting | bytes 33554432 | tf_op jit(solution)/shard_map/all_gather | solution.py:127
  526.6 17.5 %fusion.11 = f32[4,512,64,4]{2,3,1,0:T(4,128)} fusion(bf16[64,4,64,512]{2,0,3,1:T(8,128)(2,1)} %copy.68, f32[4,512,64,4]{2,3,1,0:T(4,128)} %get-tuple-element.9, f32[4,4,512]{0,2,1:T(8,128)S(1)} %broadcast_maximum_fusion, pred[64]{0:T(512)(128)(4,1)S(1)} %iota_compare_fusion), kind=kOutput, calls=%fused_computation.22 | convolution fusion | flops 69730304 | bytes 21004352 | tf_op jit(solution)/shard_map/qkhc,khdc->qhdc/dot_general | solution.py:137
  544.0 3.5 copy.69
  547.5 0.3 fusion.6
  547.8 0.0 copy-done
  547.8 2.3 multiply_reduce_fusion
  550.1 66.6 %psum.7 = f32[]{:T(128)} all-reduce(f32[]{:T(128)} %get-tuple-element.10), channel_id=1, replica_groups=mesh['scene'=8,'frame'=16] {'scene','frame'}, use_global_device_ids=true, to_apply=%region_4.5 | all-reduce | flops 1 | bytes 8 | tf_op jit(solution)/shard_map/psum | solution.py:146
  (8 shorter events, 0.1 us)
Async XLA Ops:
  7.2 540.7 %copy-start = (bf16[256,256]{1,0:T(8,128)(2,1)S(1)}, bf16[256,256]{1,0:T(8,128)(2,1)}, u32[]{:S(2)}) copy-start(bf16[256,256]{1,0:T(8,128)(2,1)} %param.17) | copy-start | bytes 393220
  7.2 472.7 %all-gather.2.cloned.1.call-start = ((), (), s32[]{:S(2)}) async-start(), calls=%async_computation.1 | async-start | bytes 17825792 | tf_op jit(solution)/shard_map/all_gather | solution.py:127
  10.5 2.9 copy-start.3
  16.0 5.0 copy-start.1
  30.8 5.8 copy-start.4
  31.2 8.9 %collective-permute-start = (bf16[1,256,512]{2,1,0:T(8,128)(2,1)S(1)}, bf16[1,256,512]{2,1,0:T(8,128)(2,1)S(1)}, u32[]{:S(2)}, u32[]{:S(2)}) collective-permute-start(bf16[1,256,512]{2,1,0:T(8,128)(2,1)S(1)} %get-tuple-element.3), channel_id=1, source_target_pairs={{0,1},{1,2},{2,3},{3,4},{4,5},{5,6},{6,7},{7,8},{8,9},{9,10},{10,1... | collective-permute-start | bytes 786440 | tf_op jit(solution)/shard_map/ppermute | solution.py:25
  35.1 8.8 %collective-permute-start.1 = (bf16[1,256,512]{2,1,0:T(8,128)(2,1)S(1)}, bf16[1,256,512]{2,1,0:T(8,128)(2,1)S(1)}, u32[]{:S(2)}, u32[]{:S(2)}) collective-permute-start(bf16[1,256,512]{2,1,0:T(8,128)(2,1)S(1)} %get-tuple-element.2), channel_id=1, source_target_pairs={{1,0},{2,1},{3,2},{4,3},{5,4},{6,5},{7,6},{8,7},{9,8},{10,9},{11,1... | collective-permute-start | bytes 786440 | tf_op jit(solution)/shard_map/ppermute | solution.py:27
  40.5 4.5 copy-start.5
  44.9 1.5 copy-start.6
  52.8 9.5 %copy-start.7 = (bf16[256,256]{1,0:T(8,128)(2,1)S(1)}, bf16[256,256]{1,0:T(8,128)(2,1)}, u32[]{:S(2)}) copy-start(bf16[256,256]{1,0:T(8,128)(2,1)} %param.14) | copy-start | bytes 393220
  52.8 319.1 %all-to-all-start = ((bf16[16,4,4,64,512]{4,3,2,1,0:T(8,128)(2,1)}), bf16[16,4,4,64,512]{4,3,2,1,0:T(8,128)(2,1)}, u32[]{:S(2)}, u32[]{:S(2)}) async-start(bf16[16,4,4,64,512]{4,3,2,1,0:T(8,128)(2,1)} %stack.3), calls=%async_computation | async-start | bytes 33554432 | tf_op jit(solution)/shard_map/all_to_all | solution.py:125
  65.3 358.5 %copy-start.2 = (bf16[4,4,64,512]{2,0,3,1:T(4,128)(2,1)S(1)}, bf16[4,4,64,512]{2,0,3,1:T(4,128)(2,1)}, u32[]{:S(2)}) copy-start(bf16[4,4,64,512]{2,0,3,1:T(4,128)(2,1)} %copy.67) | copy-start | bytes 3145732
Sparse Core Ops, SparseCore 0:
  46.5 338.1 all-gather.1
